TPU v7x, 32 devices: a whole 2x2x4 slice. The times are simulated.
32 devices in a mesh: seq: 8 (over y, x, core), head: 4 (over z).
Axes of the slice: x: 2, y: 2, z: 4, core: 2. Of those that a mesh axis runs over, the one named last changes fastest.
Arguments:
- lin_query: bfloat16 [1024, 2048], P('seq', 'head'), may hold values from -0.52734375 to 0.52734375
- lin_key: bfloat16 [1024, 2048], P('seq', 'head'), may hold values from -0.52734375 to 0.52734375
- lin_value: bfloat16 [1024, 2048], P('seq', 'head'), may hold values from -6 to 6
- log_decay: float32 [16, 1024], P('head', 'seq'), may hold values from -1.5 to 0
- out_gate: bfloat16 [1024, 2048], P('seq', 'head'), may hold values from -8 to 8
- norm_gain: float32 [2048], P('head'), may hold values from 0.25 to 1.75
- soft_query: bfloat16 [1024, 2048], P('seq', 'head'), may hold values from -8 to 8
- soft_key: bfloat16 [1024, 256], P('seq'), may hold values from -6 to 6
- soft_value: bfloat16 [1024, 256], P('seq'), may hold values from -6 to 6
- segment_of: int32 [8], replicated, may hold values from 0 to 7, each once
Outputs:
- lin_out: bfloat16 [1024, 2048], P('seq', 'head')
- soft_out: bfloat16 [1024, 2048], P('seq', 'head')
Inputs may be any that keep to these rules, and one draw needn't show every extreme that they name: `segment_of`: each segment number stands once.
All inputs are finite; a program needn't handle non-finite values.
Results may differ from a plain program's by a relative error of at most 0.008.
Values may be sent and summed in bfloat16 or wider, within the bound.
A program may use at most 128 MiB of HBM per device.

v0:
```python
import jax
import jax.numpy as jnp
from jax import lax
from jax.sharding import PartitionSpec as P

HEAD_DIM = 128
HEADS_DEV = 4
Q_PER_KV = 8


norm_eps = 1e-06


def entering(array, axis, join, neutral):
    place = lax.axis_index(axis)
    gathered = jax.tree.map(
        lambda a, kind: lax.all_gather(a.astype(kind), axis), array, (jnp.bfloat16, jnp.bfloat16)
    )
    state = jax.tree.map(lambda a, e: jnp.zeros_like(a) + jnp.asarray(e, a.dtype), array, neutral)

    def one(hop, state):
        return join(
            state,
            jax.tree.map(
                lambda a, own: lax.dynamic_index_in_dim(a, hop, 0, False).astype(own.dtype),
                gathered,
                array,
            ),
        )

    return lax.fori_loop(0, place, one, state)


def decay_weights(cumulative):
    row_count = cumulative.shape[1]
    positions = jnp.arange(row_count, dtype=jnp.int32)
    causal_mask = positions[:, None] >= positions[None, :]
    spread = cumulative[:, :, None] - cumulative[:, None, :]
    return jnp.where(causal_mask[None], jnp.exp(jnp.where(causal_mask[None], spread, 0.0)), 0.0)


def combine_memory(earlier_part, later_part):
    return (
        jnp.exp(later_part[1])[:, None, None] * earlier_part[0] + later_part[0],
        earlier_part[1] + later_part[1],
    )


def shards(
    lin_query,
    lin_key,
    lin_value,
    log_decay,
    out_gate,
    norm_gain,
    soft_query,
    soft_key,
    soft_value,
    segment_of,
):
    tokens = lin_query.shape[0]
    query_heads = lin_query.reshape(tokens, HEADS_DEV, HEAD_DIM)
    key_heads = lin_key.reshape(tokens, HEADS_DEV, HEAD_DIM)
    value_heads = lin_value.reshape(tokens, HEADS_DEV, HEAD_DIM)
    cumulative = jnp.cumsum(log_decay, axis=1)
    scores = jnp.einsum("thd,shd->hts", query_heads, key_heads, preferred_element_type=jnp.float32)
    mixing = (scores * decay_weights(cumulative)).astype(jnp.bfloat16)
    inside = jnp.einsum("hts,shd->thd", mixing, value_heads, preferred_element_type=jnp.float32)
    tail_decay = jnp.exp(cumulative[:, -1:] - cumulative)
    weighted_keys = key_heads.astype(jnp.float32) * tail_decay.T[:, :, None]
    local_memory = jnp.einsum(
        "thd,the->hde",
        weighted_keys,
        value_heads.astype(jnp.float32),
        precision=lax.Precision.HIGHEST,
    )
    block_log = cumulative[:, -1]
    memory_prev, log_prev = entering(
        (local_memory, block_log),
        "seq",
        combine_memory,
        (jnp.zeros_like(local_memory), jnp.zeros_like(block_log)),
    )
    lifted = query_heads.astype(jnp.float32) * jnp.exp(cumulative).T[:, :, None]
    earlier_term = jnp.einsum("thd,hde->the", lifted, memory_prev, precision=lax.Precision.HIGHEST)
    mixed_out = inside + earlier_term
    square_sums = jnp.sum(mixed_out * mixed_out, axis=(1, 2))
    all_squares = lax.psum(square_sums, "head")
    width_all = HEADS_DEV * HEAD_DIM * lax.axis_size("head")
    inverse_rms = lax.rsqrt(all_squares / width_all + norm_eps)
    flattened = mixed_out.reshape(tokens, HEADS_DEV * HEAD_DIM)
    lin_out = (
        flattened
        * inverse_rms[:, None]
        * norm_gain[None, :]
        * jax.nn.sigmoid(out_gate.astype(jnp.float32))
    ).astype(jnp.bfloat16)
    own_index = lax.axis_index("seq")
    segment_range = jnp.arange(segment_of.shape[0], dtype=jnp.int32)
    own_segment = jnp.sum(jnp.where(segment_range == own_index, segment_of, 0))
    local_rows = jnp.arange(tokens, dtype=jnp.int32)
    query_pos = own_segment * tokens + local_rows
    soft_heads = soft_query.reshape(tokens, HEADS_DEV, HEAD_DIM)
    score_scale = HEAD_DIM ** (-0.5)
    shared_index = lax.axis_index("head") * HEADS_DEV // Q_PER_KV
    own_keys = lax.dynamic_slice_in_dim(soft_key, shared_index * HEAD_DIM, HEAD_DIM, 1)
    own_values = lax.dynamic_slice_in_dim(soft_value, shared_index * HEAD_DIM, HEAD_DIM, 1)
    key_piece = lax.all_gather(own_keys, "seq", axis=0, tiled=True)
    value_piece = lax.all_gather(own_values, "seq", axis=0, tiled=True)
    row_count = key_piece.shape[0]
    row_ids = jnp.arange(row_count, dtype=jnp.int32)
    owners = row_ids // tokens
    key_segments = jnp.sum(
        jnp.where(owners[:, None] == segment_range[None, :], segment_of[None, :], 0), axis=1
    )
    key_pos = key_segments * tokens + row_ids % tokens
    visible = (key_pos[None, :] <= query_pos[:, None])[None]
    raw_logits = jnp.einsum(
        "tgd,sd->gts", soft_heads, key_piece, preferred_element_type=jnp.float32
    )
    old_max = jnp.full((HEADS_DEV, tokens), -1e30, jnp.float32)
    piece_max = jnp.max(jnp.where(visible, raw_logits * score_scale, -1e30), axis=2)
    new_max = jnp.maximum(old_max, piece_max)
    weights_now = jnp.where(visible, jnp.exp(raw_logits * score_scale - new_max[:, :, None]), 0.0)
    piece_total = jnp.sum(weights_now, axis=2)
    weights_low = weights_now.astype(jnp.bfloat16)
    new_acc = jnp.einsum(
        "gts,sd->gtd", weights_low, value_piece, preferred_element_type=jnp.float32
    )
    normalized = new_acc / piece_total[:, :, None]
    soft_out = (
        normalized.transpose(1, 0, 2).reshape(tokens, HEADS_DEV * HEAD_DIM).astype(jnp.bfloat16)
    )
    return (lin_out, soft_out)


def solution(mesh):
    return jax.shard_map(
        shards,
        mesh=mesh,
        in_specs=(
            P("seq", "head"),
            P("seq", "head"),
            P("seq", "head"),
            P("head", "seq"),
            P("seq", "head"),
            P("head"),
            P("seq", "head"),
            P("seq", None),
            P("seq", None),
            P(),
        ),
        out_specs=(P("seq", "head"), P("seq", "head")),
        check_vma=False,
    )
```

profile of v0, /device:TPU:7, one launch (start us, length us, event | category | flops | bytes accessed | tf_op | source)
XLA Modules:
  0.0 77.3 jit_solution(15997218738576638989)
XLA Ops:
  7.2 0.0 copy-start
  7.2 0.0 all-gather.4.cloned.1.call-start
  7.2 1.0 %reduce_window_sum.11 = f32[4,128]{1,0:T(4,128)S(1)} reduce-window(f32[4,128]{1,0:T(4,128)} %param.15, f32[]{:T(128)} %constant.75.clone.1), window={size=1x128 pad=0_0x127_0}, to_apply=%region_0.0 | reduce-window | flops 65024 | bytes 4100 | tf_op jit(solution)/shard_map/jit(cumsum)/reduce_window_sum | solution.py:65
  8.2 0.2 slice_reduce_fusion
  8.4 0.1 exponential_bitcast_fusion.1
  8.5 1.0 %copy.59 = bf16[128,512]{0,1:T(8,128)(2,1)S(1)} copy(bf16[128,512]{1,0:T(8,128)(2,1)} %param.13) | data formatting | bytes 262144 | tf_op jit(solution)/shard_map/reshape | solution.py:63
  9.5 1.8 %convolution_convert_fusion = bf16[4,128,128]{2,1,0:T(8,128)(2,1)} fusion(bf16[128,4,128]{0,2,1:T(8,128)(2,1)S(1)} %bitcast.95, f32[128,4]{0,1:T(4,128)S(1)} %get-tuple-element.66, bf16[128,512]{1,0:T(8,128)(2,1)} %param.14), kind=kOutput, calls=%fused_computation.16 | convolution fusion | flops 100859904 | bytes 395264 | tf_op jit(solution)/shard_map/thd,the->hde/dot_general | solution.py:71
  11.4 0.0 all-gather.4.cloned.1.call-update
  11.4 0.2 fusion.50
  11.6 0.8 constant_dynamic-slice_fusion
  12.4 8.8 %all_gather.19 = bf16[1024,128]{1,0:T(8,128)(2,1)S(1)} all-gather(bf16[128,128]{1,0:T(8,128)(2,1)S(1)} %constant_dynamic-slice_fusion), channel_id=1, replica_groups=mesh['seq'=8,'head'=4] {'seq'}, dimensions={0}, use_global_device_ids=true | all-gather | bytes 294912 | tf_op jit(solution)/shard_map/all_gather | solution.py:108
  21.2 1.3 %fusion.51 = s32[]{:T(128)} fusion(s32[8]{0:T(128)} %param.21, s32[]{:T(128)} %axis_index.27), kind=kLoop, calls=%fused_computation.73 | loop fusion | flops 23 | bytes 40 | tf_op jit(solution)/shard_map/reduce_sum | solution.py:100
  23.2 0.7 select_reduce_fusion
  23.9 0.8 constant_dynamic-slice_fusion.1
  24.7 0.1 copy.58
  24.8 9.9 %all_gather.20 = bf16[1024,128]{0,1:T(8,128)(2,1)S(1)} all-gather(bf16[128,128]{0,1:T(8,128)(2,1)S(1)} %copy.58), channel_id=1, replica_groups=mesh['seq'=8,'head'=4] {'seq'}, dimensions={0}, use_global_device_ids=true | all-gather | bytes 294912 | tf_op jit(solution)/shard_map/all_gather | solution.py:109
  34.6 1.2 %dynamic-slice = u32[1]{0:T(128)} dynamic-slice(u32[32]{0:T(128)} %constant.96, u32[]{:T(128)S(6)} %add.76), dynamic_slice_sizes={1} | dynamic-slice | bytes 12
  36.5 0.2 dynamic-update-slice
  36.8 11.2 %all-reduce = bf16[32]{0:T(256)(128)(2,1)S(1)} all-reduce(bf16[32]{0:T(256)(128)(2,1)S(1)} %dynamic-update-slice), channel_id=2, replica_groups=mesh['seq'=8,'head'=4] {'seq'}, use_global_device_ids=true, to_apply=%add | all-reduce | flops 32 | bytes 128
  48.0 0.2 broadcast_compare_fusion
  48.3 0.0 copy-done
  48.3 0.5 fusion
  48.7 0.5 fusion.3
  49.2 0.0 copy-start.1
  49.2 0.0 copy-start.2
  49.2 0.5 fusion.8
  49.8 0.8 copy.55
  50.5 0.1 reshape.128
  50.6 0.0 copy-done.1
  50.7 0.0 copy-done.2
  50.7 0.4 convolution_bitcast_fusion.2
  51.0 0.0 all-gather.4.cloned.1.call-done
  51.1 0.0 copy-start.3
  51.1 0.0 copy-start.4
  51.1 7.5 %while.12 = (s32[]{:T(128)}, f32[4,128,128]{2,1,0:T(8,128)S(1)}, s32[]{:T(128)}, bf16[8,4]{1,0:T(8,128)(2,1)S(1)}, bf16[8,4,128,128]{3,2,1,0:T(8,128)(2,1)}, /*index=5*/s32[]{:T(128)}, s32[]{:T(128)}, s32[]{:T(128)}) while((s32[]{:T(128)}, f32[4,128,128]{2,1,0:T(8,128)S(1)}, s32[]{:T(128)}, bf16[8,4]{1,0:T(8,128)(2,1)S(1)}, ...), condition=%wide.region_2.3_spmd, body=%wide.region_1.2_spmd.sunk | while | flops 196617 | bytes 655527 | solution.py:31
  51.2 1.0 %convert_add_fusion.2 = f32[4,128,128]{2,1,0:T(8,128)S(1)} fusion(f32[4,128,128]{2,1,0:T(8,128)S(1)} %get-tuple-element.112, bf16[8,4,128,128]{3,2,1,0:T(8,128)(2,1)} %get-tuple-element.123, s32[]{:T(128)S(6)} %select_n.93, f32[4]{0:T(128)S(1)} %exponential_bitcast_fusion.4), kind=kLoop, calls=%fused_computation.clone.1 | loop fusion | flops 196608 | bytes 655380 | tf_op jit(solution)/shard_map/while/body/add | solution.py:44
  52.2 1.0 %convert_add_fusion.2 = f32[4,128,128]{2,1,0:T(8,128)S(1)} fusion(f32[4,128,128]{2,1,0:T(8,128)S(1)} %get-tuple-element.112, bf16[8,4,128,128]{3,2,1,0:T(8,128)(2,1)} %get-tuple-element.123, s32[]{:T(128)S(6)} %select_n.93, f32[4]{0:T(128)S(1)} %exponential_bitcast_fusion.4), kind=kLoop, calls=%fused_computation.clone.1 | loop fusion | flops 196608 | bytes 655380 | tf_op jit(solution)/shard_map/while/body/add | solution.py:44
  53.3 1.0 %convert_add_fusion.2 = f32[4,128,128]{2,1,0:T(8,128)S(1)} fusion(f32[4,128,128]{2,1,0:T(8,128)S(1)} %get-tuple-element.112, bf16[8,4,128,128]{3,2,1,0:T(8,128)(2,1)} %get-tuple-element.123, s32[]{:T(128)S(6)} %select_n.93, f32[4]{0:T(128)S(1)} %exponential_bitcast_fusion.4), kind=kLoop, calls=%fused_computation.clone.1 | loop fusion | flops 196608 | bytes 655380 | tf_op jit(solution)/shard_map/while/body/add | solution.py:44
  54.4 1.0 %convert_add_fusion.2 = f32[4,128,128]{2,1,0:T(8,128)S(1)} fusion(f32[4,128,128]{2,1,0:T(8,128)S(1)} %get-tuple-element.112, bf16[8,4,128,128]{3,2,1,0:T(8,128)(2,1)} %get-tuple-element.123, s32[]{:T(128)S(6)} %select_n.93, f32[4]{0:T(128)S(1)} %exponential_bitcast_fusion.4), kind=kLoop, calls=%fused_computation.clone.1 | loop fusion | flops 196608 | bytes 655380 | tf_op jit(solution)/shard_map/while/body/add | solution.py:44
  55.4 1.0 %convert_add_fusion.2 = f32[4,128,128]{2,1,0:T(8,128)S(1)} fusion(f32[4,128,128]{2,1,0:T(8,128)S(1)} %get-tuple-element.112, bf16[8,4,128,128]{3,2,1,0:T(8,128)(2,1)} %get-tuple-element.123, s32[]{:T(128)S(6)} %select_n.93, f32[4]{0:T(128)S(1)} %exponential_bitcast_fusion.4), kind=kLoop, calls=%fused_computation.clone.1 | loop fusion | flops 196608 | bytes 655380 | tf_op jit(solution)/shard_map/while/body/add | solution.py:44
  56.5 1.0 %convert_add_fusion.2 = f32[4,128,128]{2,1,0:T(8,128)S(1)} fusion(f32[4,128,128]{2,1,0:T(8,128)S(1)} %get-tuple-element.112, bf16[8,4,128,128]{3,2,1,0:T(8,128)(2,1)} %get-tuple-element.123, s32[]{:T(128)S(6)} %select_n.93, f32[4]{0:T(128)S(1)} %exponential_bitcast_fusion.4), kind=kLoop, calls=%fused_computation.clone.1 | loop fusion | flops 196608 | bytes 655380 | tf_op jit(solution)/shard_map/while/body/add | solution.py:44
  57.5 1.0 %convert_add_fusion.2 = f32[4,128,128]{2,1,0:T(8,128)S(1)} fusion(f32[4,128,128]{2,1,0:T(8,128)S(1)} %get-tuple-element.112, bf16[8,4,128,128]{3,2,1,0:T(8,128)(2,1)} %get-tuple-element.123, s32[]{:T(128)S(6)} %select_n.93, f32[4]{0:T(128)S(1)} %exponential_bitcast_fusion.4), kind=kLoop, calls=%fused_computation.clone.1 | loop fusion | flops 196608 | bytes 655380 | tf_op jit(solution)/shard_map/while/body/add | solution.py:44
  58.6 0.7 multiply_reduce_fusion
  59.3 0.1 copy.51
  59.5 10.3 %psum.7 = f32[128]{0:T(128)S(1)} all-reduce(f32[128]{0:T(128)S(1)} %get-tuple-element.67), channel_id=1, replica_groups=mesh['seq'=8,'head'=4] {'head'}, use_global_device_ids=true, to_apply=%region_4.5 | all-reduce | flops 128 | bytes 1024 | tf_op jit(solution)/shard_map/psum | solution.py:88
  69.7 0.0 copy-done.3
  69.7 0.0 copy-done.4
  69.7 0.8 multiply_convert_fusion
  (15 shorter events, 0.1 us)
Async XLA Ops:
  7.2 41.1 %copy-start = (bf16[128,512]{1,0:T(8,128)(2,1)S(1)}, bf16[128,512]{1,0:T(8,128)(2,1)}, u32[]{:S(2)}) copy-start(bf16[128,512]{1,0:T(8,128)(2,1)} %param.18) | copy-start | bytes 393220
  7.2 43.9 %all-gather.4.cloned.1.call-start = ((), (), s32[]{:S(2)}) async-start(), calls=%async_computation | async-start | bytes 1179648 | tf_op jit(solution)/shard_map/all_gather | solution.py:17
  49.2 1.4 %copy-start.1 = (bf16[128,512]{1,0:T(8,128)(2,1)S(1)}, bf16[128,512]{1,0:T(8,128)(2,1)}, u32[]{:S(2)}) copy-start(bf16[128,512]{1,0:T(8,128)(2,1)} %param.14) | copy-start | bytes 393220
  49.2 1.4 %copy-start.2 = (bf16[128,512]{1,0:T(8,128)(2,1)S(1)}, bf16[128,512]{1,0:T(8,128)(2,1)}, u32[]{:S(2)}) copy-start(bf16[128,512]{1,0:T(8,128)(2,1)} %param.12) | copy-start | bytes 393220
  51.1 18.6 %copy-start.3 = (bf16[128,512]{1,0:T(8,128)(2,1)S(1)}, bf16[128,512]{1,0:T(8,128)(2,1)}, u32[]{:S(2)}) copy-start(bf16[128,512]{1,0:T(8,128)(2,1)} %param.16) | copy-start | bytes 393220
  51.1 18.6 %copy-start.4 = (f32[512]{0:T(512)S(1)}, f32[512]{0:T(512)}, u32[]{:S(2)}) copy-start(f32[512]{0:T(512)} %param.17) | copy-start | bytes 6148
Sparse Core Ops, SparseCore 0:
  11.5 24.8 all-gather.3
where the time goes:
time: 77.9 us; the launch traced here: 77.3 us
  blocking collectives  40.2 us (52%)
  between operations  15.5 us (20%)
  other arithmetic  11.8 us (15%)
  local copies, waits for them, and re-layouts  5.58 us (7%)
  matrix products  3.92 us (5%)
    unnamed x1, blocking collectives  11.2 us
    psum x1, blocking collectives, shards(): all_squares = lax.psum(square_sums, 'head')  10.3 us
    all_gather x1, blocking collectives, shards(): value_piece = lax.all_gather(own_values, 'seq', axis=0, tiled=True)  9.86 us
    all_gather x1, blocking collectives, shards(): key_piece = lax.all_gather(own_keys, 'seq', axis=0, tiled=True)  8.83 us
    add x7, other arithmetic, combine_memory(): jnp.exp(later_part[1])[:, None, None] * earlier_part[0] + later_part[0]  7.14 us
    unnamed x15, local copies, waits for them, and re-layouts  2.41 us
    dot_general x1, matrix products, shards(): jnp.einsum('thd,the->hde', weighted_keys, value_heads.astype(jnp.float32)...  1.83 us
  transfers between devices with their start and end apart: 1, of which 0 were waited for; matrix products, arithmetic and copies ran while one was open for 11% of the time, Pallas kernels for 0%

commit v1 on v0

v1 whole, which is shorter than its diff:
```python
import functools

import jax
import jax.numpy as jnp
from jax import lax
from jax.experimental import pallas as pl
from jax.experimental.pallas import tpu as pltpu
from jax.sharding import PartitionSpec as P

HEAD_DIM = 128
Q_PER_KV = 8
NORM_EPS = 1e-06
MESH = pl.DeviceIdType.MESH
F32 = jnp.float32
BF16 = jnp.bfloat16
NT = (((1,), (1,)), ((), ()))
TN = (((0,), (0,)), ((), ()))
HIGH = lax.Precision.HIGHEST


def dot(a, b, dims=(((1,), (0,)), ((), ())), precision=None):
    return lax.dot_general(a, b, dims, preferred_element_type=F32, precision=precision)


def each(count, body):
    if count <= 8:
        for i in range(count):
            body(i)
    else:
        lax.fori_loop(0, count, lambda i, _: (body(i), 0)[1], 0)


def kernel(
    n,
    nh,
    lq_hbm,
    lk_hbm,
    lv_hbm,
    ld_hbm,
    gate_hbm,
    gain_ref,
    sq_hbm,
    sk_hbm,
    sv_hbm,
    seg_ref,
    lin_ref,
    soft_ref,
    lq,
    lk,
    lv,
    gate,
    sq,
    qs,
    kv,
    logs,
    mem_own,
    mem_sib,
    tot_own,
    tot_all,
    pre,
    ent_own,
    ent_sib,
    mixed,
    sums,
    top,
    acc,
    den,
    in_sem,
    kv_send,
    kv_recv,
    fwd_send,
    log_send,
    log_recv,
    mem_send,
    mem_recv,
    tot_send,
    tot_recv,
    ent_send,
    ent_recv,
    sum_send,
    sum_recv,
):
    chips = n // 2
    me = lax.axis_index("seq")
    col = lax.axis_index("head")
    chip, core = me // 2, me % 2
    sib = chip * 2 + 1 - core
    tokens = lq.shape[0]
    heads = lq.shape[1] // HEAD_DIM
    half = heads // 2
    share = pl.multiple_of((col * heads // Q_PER_KV) * HEAD_DIM, HEAD_DIM)

    barrier = pltpu.get_barrier_semaphore()

    def greet(i):
        pl.semaphore_signal(
            barrier, inc=1, device_id=((me + 1 + i) % n, col), device_id_type=MESH
        )

    def greet_col(i):
        pl.semaphore_signal(
            barrier, inc=1, device_id=(me, (col + 1 + i) % nh), device_id_type=MESH
        )

    each(n - 1, greet)
    each(nh - 1, greet_col)

    def local(src, dst, at):
        copy = pltpu.make_async_copy(src, dst, in_sem.at[at])
        copy.start()
        return copy

    get_ld = local(ld_hbm, logs.at[me], 0)
    get_lk = local(lk_hbm, lk, 1)
    get_lv = local(lv_hbm, lv, 2)
    get_lq = local(lq_hbm, lq, 3)
    get_sk = local(sk_hbm.at[:, pl.ds(share, HEAD_DIM)], kv.at[me, 0], 4)
    get_sv = local(sv_hbm.at[:, pl.ds(share, HEAD_DIM)], kv.at[me, 1], 5)
    get_sq = local(sq_hbm, sq, 6)
    get_gate = local(gate_hbm, gate, 7)

    def remote(src, dst, send, recv, seq_to, col_to):
        return pltpu.make_async_remote_copy(
            src_ref=src,
            dst_ref=dst,
            send_sem=send,
            recv_sem=recv,
            device_id=(seq_to, col_to),
            device_id_type=MESH,
        )

    get_ld.wait()
    get_sk.wait()
    get_sv.wait()
    pl.semaphore_wait(barrier, n - 1 + nh - 1)

    def log_copy(i):
        return remote(
            logs.at[me],
            logs.at[me],
            log_send.at[i],
            log_recv.at[i],
            (me + 1 + i) % n,
            col,
        )

    def kv_copy(i, part, to):
        return remote(
            kv.at[me, part],
            kv.at[me, part],
            kv_send.at[i, part],
            kv_recv.at[i, part],
            to,
            col,
        )

    def far(i):
        return ((chip + 1 + i) % chips) * 2 + core

    def near(i):
        return (chip + chips - 1 - i) % chips

    each(n - 1, lambda i: log_copy(i).start())

    def kv_go(i):
        kv_copy(i, 0, far(i)).start()
        kv_copy(i, 1, far(i)).start()

    each(chips - 1, kv_go)
    kv_copy(chips - 1, 0, sib).start()
    kv_copy(chips - 1, 1, sib).start()

    rows = lax.broadcasted_iota(jnp.int32, (tokens, tokens), 0)
    cols = lax.broadcasted_iota(jnp.int32, (tokens, tokens), 1)
    causal = rows >= cols
    lower = jnp.where(causal, 1.0, 0.0).astype(F32)
    decay = logs[me]
    cum_row = dot(decay, lower, NT, HIGH)
    cum_col = dot(lower, decay, NT, HIGH)
    tail = jnp.exp(cum_col[tokens - 1 : tokens, :] - cum_col)
    lift = jnp.exp(cum_col)

    def cut(h):
        return slice(h * HEAD_DIM, (h + 1) * HEAD_DIM)

    get_lk.wait()
    get_lv.wait()
    for h in range(heads):
        weighted = (lk[:, cut(h)].astype(F32) * tail[:, h : h + 1]).astype(BF16)
        mem_own[h] = dot(weighted, lv[:, cut(h)], TN).astype(BF16)
    mem_copy = remote(mem_own, mem_sib, mem_send, mem_recv, sib, col)
    mem_copy.start()

    get_lq.wait()
    for h in range(heads):
        scores = dot(lq[:, cut(h)], lk[:, cut(h)], NT)
        spread = cum_col[:, h : h + 1] - cum_row[h : h + 1, :]
        weight = jnp.where(causal, jnp.exp(jnp.where(causal, spread, 0.0)), 0.0)
        mixing = (scores * weight).astype(BF16)
        mixed[:, cut(h)] = dot(mixing, lv[:, cut(h)])

    each(n - 1, lambda i: log_copy(i).wait_recv())

    def total(i):
        return jnp.sum(logs[i], axis=1, keepdims=True)

    odd_decay = jnp.exp(total(chip * 2 + 1))
    first = core.astype(F32)
    mem_copy.wait_recv()
    for p in range(half):
        h = core * half + p
        factor = jnp.where(core == 0, odd_decay[p : p + 1], odd_decay[half + p : half + p + 1])
        mine = mem_own[h].astype(F32)
        other = mem_sib[h].astype(F32)
        early = jnp.where(first > 0.5, other, mine)
        late = jnp.where(first > 0.5, mine, other)
        tot_own[p] = (factor * early + late).astype(BF16)

    def tot_copy(i):
        return remote(
            tot_own,
            tot_all.at[chip],
            tot_send.at[i],
            tot_recv.at[chip],
            i * 2 + core,
            col,
        )

    def tot_go(i):
        @pl.when(i > chip)
        def _():
            tot_copy(i).start()

    each(chips, tot_go)

    scale = HEAD_DIM ** (-0.5)
    own_segment = seg_ref[me]
    get_sq.wait()
    for h in range(heads):
        qs[h * tokens : (h + 1) * tokens, :] = sq[:, cut(h)]

    def soft_first():
        logits = dot(qs[...], kv[me, 0], NT) * scale
        shape = (heads, tokens, tokens)
        logits = jnp.where(causal[None], logits.reshape(shape), -1e30).reshape(
            heads * tokens, tokens
        )
        peak = jnp.max(logits, axis=1, keepdims=True)
        weights = jnp.exp(logits - peak)
        top[...] = peak
        den[...] = jnp.sum(weights, axis=1, keepdims=True)
        acc[...] = dot(weights.astype(BF16), kv[me, 1])

    def soft_next(owner):
        shown = seg_ref[owner] < own_segment
        bias = jnp.where(shown, 0.0, -1e30).astype(F32)
        logits = dot(qs[...], kv[owner, 0], NT) * scale + bias
        old = top[...]
        peak = jnp.maximum(old, jnp.max(logits, axis=1, keepdims=True))
        fade = jnp.exp(old - peak)
        weights = jnp.exp(logits - peak)
        top[...] = peak
        den[...] = den[...] * fade + jnp.sum(weights, axis=1, keepdims=True)
        acc[...] = acc[...] * fade + dot(weights.astype(BF16), kv[owner, 1])

    soft_first()

    def fwd_copy(i, part, owner):
        return remote(
            kv.at[owner, part],
            kv.at[owner, part],
            fwd_send.at[i, part],
            kv_recv.at[chips + i, part],
            sib,
            col,
        )

    def kv_pass(i):
        owner = near(i) * 2 + core
        for part in range(2):
            kv_copy(i, part, far(i)).wait_recv()
            fwd_copy(i, part, owner).start()
        soft_next(owner)

    each(chips - 1, kv_pass)

    pre[...] = jnp.zeros_like(pre)

    def join(i):
        @pl.when(i < chip)
        def _():
            remote(tot_own, tot_all.at[i], tot_send.at[i], tot_recv.at[i], sib, col).wait_recv()
            both = jnp.exp(total(i * 2) + total(i * 2 + 1))
            for p in range(half):
                factor = jnp.where(core == 0, both[p : p + 1], both[half + p : half + p + 1])
                pre[p] = factor * pre[p] + tot_all[i, p].astype(F32)

    each(chips, join)
    ent_own[...] = pre[...].astype(BF16)
    ent_copy = remote(ent_own, ent_sib, ent_send, ent_recv, sib, col)
    ent_copy.start()

    kv_copy(chips - 1, 0, sib).wait_recv()
    kv_copy(chips - 1, 1, sib).wait_recv()
    soft_next(sib)

    even_decay = jnp.exp(total(chip * 2))
    ent_copy.wait_recv()
    squares = jnp.zeros((tokens, HEAD_DIM), F32)
    for h in range(heads):
        pair, p = h // half, h % half
        here = jnp.where(core == pair, ent_own[p].astype(F32), ent_sib[p].astype(F32))
        later = even_decay[h : h + 1] * here + mem_sib[h].astype(F32)
        state = jnp.where(core == 0, here, later).astype(BF16)
        lifted = (lq[:, cut(h)].astype(F32) * lift[:, h : h + 1]).astype(BF16)
        value = mixed[:, cut(h)] + dot(lifted, state)
        mixed[:, cut(h)] = value
        squares = squares + value * value
    sums[col] = dot(jnp.ones((8, HEAD_DIM), F32), squares, NT, HIGH)

    def sum_copy(i):
        return remote(
            sums.at[col],
            sums.at[col],
            sum_send.at[i],
            sum_recv.at[i],
            me,
            (col + 1 + i) % nh,
        )

    each(nh - 1, lambda i: sum_copy(i).start())

    def kv_last(i):
        for part in range(2):
            fwd_copy(i, part, near(i) * 2 + core).wait_recv()
        soft_next(near(i) * 2 + 1 - core)

    each(chips - 1, kv_last)
    for h in range(heads):
        r = slice(h * tokens, (h + 1) * tokens)
        soft_ref[:, cut(h)] = (acc[r, :] / den[r, :]).astype(BF16)

    get_gate.wait()
    each(nh - 1, lambda i: sum_copy(i).wait_recv())
    everyone = sums[...].reshape(nh * 8, tokens)
    eighth = jnp.full((nh * 8, HEAD_DIM), 0.125, F32)
    spread_sums = dot(everyone, eighth, TN, HIGH)
    inverse = lax.rsqrt(spread_sums / (heads * HEAD_DIM * nh) + NORM_EPS)
    for h in range(heads):
        opened = jax.nn.sigmoid(gate[:, cut(h)].astype(F32))
        lin_ref[:, cut(h)] = (mixed[:, cut(h)] * inverse * gain_ref[:, cut(h)] * opened).astype(
            BF16
        )

    each(n - 1, lambda i: log_copy(i).wait_send())

    def kv_sent(i):
        for part in range(2):
            kv_copy(i, part, sib).wait_send()

    each(chips, kv_sent)

    def fwd_sent(i):
        for part in range(2):
            fwd_copy(i, part, near(i) * 2 + core).wait_send()

    each(chips - 1, fwd_sent)
    mem_copy.wait_send()

    def tot_sent(i):
        @pl.when(i > chip)
        def _():
            tot_copy(i).wait_send()

    each(chips, tot_sent)
    ent_copy.wait_send()
    each(nh - 1, lambda i: sum_copy(i).wait_send())


def solution(mesh):
    n, nh = mesh.shape["seq"], mesh.shape["head"]
    chips = n // 2

    def step(lq, lk, lv, ld, gate, gain, sq, sk, sv, seg):
        tokens, width = lq.shape
        heads = width // HEAD_DIM
        half = heads // 2
        block = (tokens, width)
        square = (HEAD_DIM, HEAD_DIM)
        dma = pltpu.SemaphoreType.DMA
        anywhere = pl.BlockSpec(memory_space=pl.ANY)
        vmem = pl.BlockSpec(memory_space=pltpu.VMEM)
        return pl.pallas_call(
            functools.partial(kernel, n, nh),
            out_shape=[jax.ShapeDtypeStruct(block, BF16)] * 2,
            in_specs=[anywhere] * 5
            + [vmem]
            + [anywhere] * 3
            + [pl.BlockSpec(memory_space=pltpu.SMEM)],
            out_specs=[vmem, vmem],
            scratch_shapes=[
                pltpu.VMEM(block, BF16),
                pltpu.VMEM(block, BF16),
                pltpu.VMEM(block, BF16),
                pltpu.VMEM(block, BF16),
                pltpu.VMEM(block, BF16),
                pltpu.VMEM((heads * tokens, HEAD_DIM), BF16),
                pltpu.VMEM((n, 2, tokens, HEAD_DIM), BF16),
                pltpu.VMEM((n, heads, tokens), F32),
                pltpu.VMEM((heads,) + square, BF16),
                pltpu.VMEM((heads,) + square, BF16),
                pltpu.VMEM((half,) + square, BF16),
                pltpu.VMEM((chips, half) + square, BF16),
                pltpu.VMEM((half,) + square, F32),
                pltpu.VMEM((half,) + square, BF16),
                pltpu.VMEM((half,) + square, BF16),
                pltpu.VMEM(block, F32),
                pltpu.VMEM((nh, 8, tokens), F32),
                pltpu.VMEM((heads * tokens, 1), F32),
                pltpu.VMEM((heads * tokens, HEAD_DIM), F32),
                pltpu.VMEM((heads * tokens, 1), F32),
                dma((8,)),
                dma((chips, 2)),
                dma((2 * chips, 2)),
                dma((chips, 2)),
                dma((n,)),
                dma((n,)),
                dma,
                dma,
                dma((chips,)),
                dma((chips,)),
                dma,
                dma,
                dma((nh,)),
                dma((nh,)),
            ],
            compiler_params=pltpu.CompilerParams(
                collective_id=0,
                has_side_effects=True,
                vmem_limit_bytes=40 * 1024 * 1024,
            ),
        )(lq, lk, lv, ld, gate, gain.reshape(1, width), sq, sk, sv, seg)

    return jax.shard_map(
        step,
        mesh=mesh,
        in_specs=(
            P("seq", "head"),
            P("seq", "head"),
            P("seq", "head"),
            P("head", "seq"),
            P("seq", "head"),
            P("head"),
            P("seq", "head"),
            P("seq", None),
            P("seq", None),
            P(),
        ),
        out_specs=(P("seq", "head"), P("seq", "head")),
        check_vma=False,
    )
```

time: 77.9 us -> 28.9 us (0.37)
  blocking collectives: 40.2 us -> 0 us
  Pallas kernels: 0 us -> 18.4 us
  between operations: 15.5 us -> 0.66 us
  other arithmetic: 11.8 us -> 0 us
  local copies, waits for them, and re-layouts: 5.58 us -> 9.52 us
  matrix products: 3.92 us -> 0 us
    all_gather x2 -> x0, blocking collectives: 18.7 us -> none  [the longest x1 9.86 us: shards(): value_piece = lax.all_gather(own_values, 'seq', axis=0, tiled=True)]
    pallas_call x0 -> x1, Pallas kernels: none -> 18.4 us  [step(): pl.pallas_call(functools.partial(kernel, n, nh), out_shape=[jax.ShapeDtyp...]
    unnamed x1 -> x0, blocking collectives: 11.2 us -> none
    psum x1 -> x0, blocking collectives: 10.3 us -> none  [shards(): all_squares = lax.psum(square_sums, 'head')]
    add x9 -> x0, other arithmetic: 7.15 us -> none  [the longest x7 7.14 us: combine_memory(): jnp.exp(later_part[1])[:, None, None] * earlier_part[0] + later_part[0]]
    unnamed x15 -> x22, local copies, waits for them, and re-layouts: 2.41 us -> 9.52 us
    dot_general x5 -> x0, matrix products: 3.92 us -> none  [the longest x1 1.83 us: shards(): jnp.einsum('thd,the->hde', weighted_keys, value_heads.astype(jnp.float32)...]
    reduce_sum x3 -> x0, other arithmetic: 2.49 us -> none  [the longest x1 1.29 us: shards(): own_segment = jnp.sum(jnp.where(segment_range == own_index, segment_of, 0))]
  transfers between devices with their start and end apart: 1 -> 0, of which waited for: 0 -> 0; matrix products, arithmetic and copies ran while one was open for 11% -> 0% of each run, Pallas kernels for 0% -> 0%
where the time goes in v1:
time: 28.9 us; the launch traced here: 28.6 us
  Pallas kernels  18.4 us (64%)
  local copies, waits for them, and re-layouts  9.52 us (33%)
  between operations  0.66 us (2%)
    pallas_call x1, Pallas kernels, step(): pl.pallas_call(functools.partial(kernel, n, nh), out_shape=[jax.ShapeDtyp...  18.4 us
    unnamed x22, local copies, waits for them, and re-layouts  9.52 us

profile of v1, /device:TPU:7, one launch (start us, length us, event | category | flops | bytes accessed | tf_op | source)
XLA Modules:
  0.0 28.6 jit_solution(16874056544070382549)
XLA Ops:
  0.6 0.0 copy-start.9
  0.6 0.6 %copy-done.9 = s32[8]{0:T(128)S(1)} copy-done((s32[8]{0:T(128)S(1)}, s32[8]{0:T(128)}, u32[]{:S(2)}) %copy-start.9) | copy-done | bytes 56
  1.3 0.0 copy-start
  1.3 0.9 %copy-done = bf16[128,512]{1,0:T(8,128)(2,1)S(1)} copy-done((bf16[128,512]{1,0:T(8,128)(2,1)S(1)}, bf16[128,512]{1,0:T(8,128)(2,1)}, u32[]{:S(2)}) %copy-start) | copy-done | bytes 131096
  2.2 0.0 copy-start.1
  2.2 0.9 %copy-done.1 = bf16[128,512]{1,0:T(8,128)(2,1)S(1)} copy-done((bf16[128,512]{1,0:T(8,128)(2,1)S(1)}, bf16[128,512]{1,0:T(8,128)(2,1)}, u32[]{:S(2)}) %copy-start.1) | copy-done | bytes 131096
  3.1 0.0 copy-start.2
  3.1 0.9 %copy-done.2 = bf16[128,512]{1,0:T(8,128)(2,1)S(1)} copy-done((bf16[128,512]{1,0:T(8,128)(2,1)S(1)}, bf16[128,512]{1,0:T(8,128)(2,1)}, u32[]{:S(2)}) %copy-start.2) | copy-done | bytes 131096
  4.0 0.0 copy-start.3
  4.0 0.9 %copy-done.3 = bf16[128,512]{1,0:T(8,128)(2,1)S(1)} copy-done((bf16[128,512]{1,0:T(8,128)(2,1)S(1)}, bf16[128,512]{1,0:T(8,128)(2,1)}, u32[]{:S(2)}) %copy-start.3) | copy-done | bytes 131096
  4.9 0.0 copy-start.4
  4.9 0.9 %copy-done.4 = bf16[128,512]{1,0:T(8,128)(2,1)S(1)} copy-done((bf16[128,512]{1,0:T(8,128)(2,1)S(1)}, bf16[128,512]{1,0:T(8,128)(2,1)}, u32[]{:S(2)}) %copy-start.4) | copy-done | bytes 131096
  5.8 0.0 copy-start.5
  5.8 0.8 %copy-done.5 = bf16[128,256]{1,0:T(8,128)(2,1)S(1)} copy-done((bf16[128,256]{1,0:T(8,128)(2,1)S(1)}, bf16[128,256]{1,0:T(8,128)(2,1)}, u32[]{:S(2)}) %copy-start.5) | copy-done | bytes 65560
  6.7 0.0 copy-start.6
  6.7 0.8 %copy-done.6 = bf16[128,256]{1,0:T(8,128)(2,1)S(1)} copy-done((bf16[128,256]{1,0:T(8,128)(2,1)S(1)}, bf16[128,256]{1,0:T(8,128)(2,1)}, u32[]{:S(2)}) %copy-start.6) | copy-done | bytes 65560
  7.5 0.0 copy-start.7
  7.5 0.7 %copy-done.7 = f32[4,128]{1,0:T(4,128)S(1)} copy-done((f32[4,128]{1,0:T(4,128)S(1)}, f32[4,128]{1,0:T(4,128)}, u32[]{:S(2)}) %copy-start.7) | copy-done | bytes 2072
  8.2 0.0 copy-start.8
  8.2 0.7 %copy-done.8 = f32[512]{0:T(512)S(1)} copy-done((f32[512]{0:T(512)S(1)}, f32[512]{0:T(512)}, u32[]{:S(2)}) %copy-start.8) | copy-done | bytes 2072
  8.9 18.4 %shard_map.113 = (bf16[128,512]{1,0:T(8,128)(2,1)S(1)}, bf16[128,512]{1,0:T(8,128)(2,1)S(1)}) custom-call(bf16[128,512]{1,0:T(8,128)(2,1)S(1)} %copy-done, bf16[128,512]{1,0:T(8,128)(2,1)S(1)} %copy-done.1, bf16[128,512]{1,0:T(8,128)(2,1)S(1)} %copy-done.2, f32[4,128]{1,0:T(4,128)S(1)} %copy-done.7, bf16[128,512]{1,0:T(8,128)(2,1)S(1)} %copy-done.3, ...), custom_call_target="tpu_custom_call" | custom-call | tf_op jit(solution)/shard_map/pallas_call | solution.py:393
  27.3 0.7 %copy.14 = bf16[128,512]{1,0:T(8,128)(2,1)} copy(bf16[128,512]{1,0:T(8,128)(2,1)S(1)} %get-tuple-element.4) | data formatting | bytes 262144
  27.9 0.7 %copy.15 = bf16[128,512]{1,0:T(8,128)(2,1)} copy(bf16[128,512]{1,0:T(8,128)(2,1)S(1)} %get-tuple-element.5) | data formatting | bytes 262144
Async XLA Ops:
  0.6 0.7 %copy-start.9 = (s32[8]{0:T(128)S(1)}, s32[8]{0:T(128)}, u32[]{:S(2)}) copy-start(s32[8]{0:T(128)} %seg_ref.1) | copy-start | bytes 100
  1.3 0.9 %copy-start = (bf16[128,512]{1,0:T(8,128)(2,1)S(1)}, bf16[128,512]{1,0:T(8,128)(2,1)}, u32[]{:S(2)}) copy-start(bf16[128,512]{1,0:T(8,128)(2,1)} %lq_hbm.1) | copy-start | bytes 393220
  2.2 0.9 %copy-start.1 = (bf16[128,512]{1,0:T(8,128)(2,1)S(1)}, bf16[128,512]{1,0:T(8,128)(2,1)}, u32[]{:S(2)}) copy-start(bf16[128,512]{1,0:T(8,128)(2,1)} %lk_hbm.1) | copy-start | bytes 393220
  3.1 0.9 %copy-start.2 = (bf16[128,512]{1,0:T(8,128)(2,1)S(1)}, bf16[128,512]{1,0:T(8,128)(2,1)}, u32[]{:S(2)}) copy-start(bf16[128,512]{1,0:T(8,128)(2,1)} %lv_hbm.1) | copy-start | bytes 393220
  4.0 0.9 %copy-start.3 = (bf16[128,512]{1,0:T(8,128)(2,1)S(1)}, bf16[128,512]{1,0:T(8,128)(2,1)}, u32[]{:S(2)}) copy-start(bf16[128,512]{1,0:T(8,128)(2,1)} %gate_hbm.1) | copy-start | bytes 393220
  4.9 0.9 %copy-start.4 = (bf16[128,512]{1,0:T(8,128)(2,1)S(1)}, bf16[128,512]{1,0:T(8,128)(2,1)}, u32[]{:S(2)}) copy-start(bf16[128,512]{1,0:T(8,128)(2,1)} %sq_hbm.1) | copy-start | bytes 393220
  5.8 0.8 %copy-start.5 = (bf16[128,256]{1,0:T(8,128)(2,1)S(1)}, bf16[128,256]{1,0:T(8,128)(2,1)}, u32[]{:S(2)}) copy-start(bf16[128,256]{1,0:T(8,128)(2,1)} %sk_hbm.1) | copy-start | bytes 196612
  6.7 0.8 %copy-start.6 = (bf16[128,256]{1,0:T(8,128)(2,1)S(1)}, bf16[128,256]{1,0:T(8,128)(2,1)}, u32[]{:S(2)}) copy-start(bf16[128,256]{1,0:T(8,128)(2,1)} %sv_hbm.1) | copy-start | bytes 196612
  7.5 0.7 %copy-start.7 = (f32[4,128]{1,0:T(4,128)S(1)}, f32[4,128]{1,0:T(4,128)}, u32[]{:S(2)}) copy-start(f32[4,128]{1,0:T(4,128)} %ld_hbm.1) | copy-start | bytes 6148
  8.2 0.7 %copy-start.8 = (f32[512]{0:T(512)S(1)}, f32[512]{0:T(512)}, u32[]{:S(2)}) copy-start(f32[512]{0:T(512)} %param.15) | copy-start | bytes 6148

commit v2 on v1

--- a/solution.py
+++ b/solution.py
@@ -38,11 +38,11 @@
     lv_hbm,
     ld_hbm,
     gate_hbm,
-    gain_ref,
+    gain_hbm,
     sq_hbm,
     sk_hbm,
     sv_hbm,
-    seg_ref,
+    seg_hbm,
     lin_ref,
     soft_ref,
     lq,
@@ -65,6 +65,8 @@
     top,
     acc,
     den,
+    gain_ref,
+    seg_ref,
     in_sem,
     kv_send,
     kv_recv,
@@ -118,6 +120,8 @@
     get_sv = local(sv_hbm.at[:, pl.ds(share, HEAD_DIM)], kv.at[me, 1], 5)
     get_sq = local(sq_hbm, sq, 6)
     get_gate = local(gate_hbm, gate, 7)
+    get_gain = local(gain_hbm, gain_ref, 8)
+    get_seg = local(seg_hbm, seg_ref, 9)
 
     def remote(src, dst, send, recv, seq_to, col_to):
         return pltpu.make_async_remote_copy(
@@ -234,6 +238,7 @@
     each(chips, tot_go)
 
     scale = HEAD_DIM ** (-0.5)
+    get_seg.wait()
     own_segment = seg_ref[me]
     get_sq.wait()
     for h in range(heads):
@@ -338,9 +343,11 @@
     each(chips - 1, kv_last)
     for h in range(heads):
         r = slice(h * tokens, (h + 1) * tokens)
-        soft_ref[:, cut(h)] = (acc[r, :] / den[r, :]).astype(BF16)
+        sq[:, cut(h)] = (acc[r, :] / den[r, :]).astype(BF16)
+    put_soft = local(sq, soft_ref, 10)
 
     get_gate.wait()
+    get_gain.wait()
     each(nh - 1, lambda i: sum_copy(i).wait_recv())
     everyone = sums[...].reshape(nh * 8, tokens)
     eighth = jnp.full((nh * 8, HEAD_DIM), 0.125, F32)
@@ -348,9 +355,11 @@
     inverse = lax.rsqrt(spread_sums / (heads * HEAD_DIM * nh) + NORM_EPS)
     for h in range(heads):
         opened = jax.nn.sigmoid(gate[:, cut(h)].astype(F32))
-        lin_ref[:, cut(h)] = (mixed[:, cut(h)] * inverse * gain_ref[:, cut(h)] * opened).astype(
+        lq[:, cut(h)] = (mixed[:, cut(h)] * inverse * gain_ref[:, cut(h)] * opened).astype(
             BF16
         )
+
+    put_lin = local(lq, lin_ref, 11)
 
     each(n - 1, lambda i: log_copy(i).wait_send())
 
@@ -375,6 +384,17 @@
     each(chips, tot_sent)
     ent_copy.wait_send()
     each(nh - 1, lambda i: sum_copy(i).wait_send())
+    put_soft.wait()
+    put_lin.wait()
+
+
+def deliver(lin_in, soft_in, lin_out, soft_out, sem):
+    first = pltpu.make_async_copy(lin_in, lin_out, sem.at[0])
+    second = pltpu.make_async_copy(soft_in, soft_out, sem.at[1])
+    first.start()
+    second.start()
+    first.wait()
+    second.wait()
 
 
 def solution(mesh):
@@ -388,16 +408,12 @@
         block = (tokens, width)
         square = (HEAD_DIM, HEAD_DIM)
         dma = pltpu.SemaphoreType.DMA
-        anywhere = pl.BlockSpec(memory_space=pl.ANY)
-        vmem = pl.BlockSpec(memory_space=pltpu.VMEM)
-        return pl.pallas_call(
+        anywhere = pl.BlockSpec(memory_space=pltpu.HBM)
+        results = pl.pallas_call(
             functools.partial(kernel, n, nh),
             out_shape=[jax.ShapeDtypeStruct(block, BF16)] * 2,
-            in_specs=[anywhere] * 5
-            + [vmem]
-            + [anywhere] * 3
-            + [pl.BlockSpec(memory_space=pltpu.SMEM)],
-            out_specs=[vmem, vmem],
+            in_specs=[anywhere] * 10,
+            out_specs=[anywhere] * 2,
             scratch_shapes=[
                 pltpu.VMEM(block, BF16),
                 pltpu.VMEM(block, BF16),
@@ -419,7 +435,9 @@
                 pltpu.VMEM((heads * tokens, 1), F32),
                 pltpu.VMEM((heads * tokens, HEAD_DIM), F32),
                 pltpu.VMEM((heads * tokens, 1), F32),
-                dma((8,)),
+                pltpu.VMEM((1, width), F32),
+                pltpu.SMEM((n,), jnp.int32),
+                dma((12,)),
                 dma((chips, 2)),
                 dma((2 * chips, 2)),
                 dma((chips, 2)),
@@ -437,9 +455,16 @@
             compiler_params=pltpu.CompilerParams(
                 collective_id=0,
                 has_side_effects=True,
-                vmem_limit_bytes=40 * 1024 * 1024,
+                vmem_limit_bytes=63 * 1024 * 1024,
             ),
         )(lq, lk, lv, ld, gate, gain.reshape(1, width), sq, sk, sv, seg)
+        return pl.pallas_call(
+            deliver,
+            out_shape=[jax.ShapeDtypeStruct(block, BF16)] * 2,
+            in_specs=[anywhere] * 2,
+            out_specs=[anywhere] * 2,
+            scratch_shapes=[dma((2,))],
+        )(*results)
 
     return jax.shard_map(
         step,

time: 28.9 us -> 28.4 us (0.983)
  local copies, waits for them, and re-layouts: 9.52 us -> 0 us
  Pallas kernels: 18.4 us -> 27.6 us
    unnamed x22 -> x0, local copies, waits for them, and re-layouts: 9.52 us -> none
    pallas_call x0 -> x1, Pallas kernels: none -> 9.06 us  [step(): pl.pallas_call(deliver, out_shape=[jax.ShapeDtypeStruct(block, BF16)] * 2...]
where the time goes in v2:
time: 28.4 us; the launch traced here: 28.2 us
  Pallas kernels  27.6 us (97%)
  between operations  0.64 us (2%)
    pallas_call x1, Pallas kernels, step(): pl.pallas_call(functools.partial(kernel, n, nh), out_shape=[jax.ShapeDtyp...  18.5 us
    pallas_call x1, Pallas kernels, step(): pl.pallas_call(deliver, out_shape=[jax.ShapeDtypeStruct(block, BF16)] * 2...  9.06 us

profile of v2, /device:TPU:7, one launch (start us, length us, event | category | flops | bytes accessed | tf_op | source)
XLA Modules:
  0.0 28.2 jit_solution(16063668239969445214)
XLA Ops:
  0.6 18.5 %shard_map.113 = (bf16[128,512]{1,0:T(8,128)(2,1)}, bf16[128,512]{1,0:T(8,128)(2,1)}) custom-call(bf16[128,512]{1,0:T(8,128)(2,1)} %lq_hbm.1, bf16[128,512]{1,0:T(8,128)(2,1)} %lk_hbm.1, bf16[128,512]{1,0:T(8,128)(2,1)} %lv_hbm.1, f32[4,128]{1,0:T(4,128)} %ld_hbm.1, bf16[128,512]{1,0:T(8,128)(2,1)} %gate_hbm.1, f32[1,512]{1,0:T(1,128)} %bitcast.1, ...), custom_call_target="tpu_custom_call" | custom-call | tf_op jit(solution)/shard_map/pallas_call | solution.py:412
  19.2 9.1 %shard_map.114 = (bf16[128,512]{1,0:T(8,128)(2,1)}, bf16[128,512]{1,0:T(8,128)(2,1)}) custom-call(bf16[128,512]{1,0:T(8,128)(2,1)} %get-tuple-element.4.lin_in, bf16[128,512]{1,0:T(8,128)(2,1)} %get-tuple-element.5.soft_in), custom_call_target="tpu_custom_call" | custom-call | tf_op jit(solution)/shard_map/pallas_call | solution.py:461

commit v3 on v1

--- a/solution.py
+++ b/solution.py
@@ -38,11 +38,11 @@
     lv_hbm,
     ld_hbm,
     gate_hbm,
-    gain_ref,
+    gain_hbm,
     sq_hbm,
     sk_hbm,
     sv_hbm,
-    seg_ref,
+    seg_hbm,
     lin_ref,
     soft_ref,
     lq,
@@ -65,6 +65,8 @@
     top,
     acc,
     den,
+    gain_ref,
+    seg_ref,
     in_sem,
     kv_send,
     kv_recv,
@@ -118,6 +120,8 @@
     get_sv = local(sv_hbm.at[:, pl.ds(share, HEAD_DIM)], kv.at[me, 1], 5)
     get_sq = local(sq_hbm, sq, 6)
     get_gate = local(gate_hbm, gate, 7)
+    get_gain = local(gain_hbm, gain_ref, 8)
+    get_seg = local(seg_hbm, seg_ref, 9)
 
     def remote(src, dst, send, recv, seq_to, col_to):
         return pltpu.make_async_remote_copy(
@@ -234,6 +238,7 @@
     each(chips, tot_go)
 
     scale = HEAD_DIM ** (-0.5)
+    get_seg.wait()
     own_segment = seg_ref[me]
     get_sq.wait()
     for h in range(heads):
@@ -341,6 +346,7 @@
         soft_ref[:, cut(h)] = (acc[r, :] / den[r, :]).astype(BF16)
 
     get_gate.wait()
+    get_gain.wait()
     each(nh - 1, lambda i: sum_copy(i).wait_recv())
     everyone = sums[...].reshape(nh * 8, tokens)
     eighth = jnp.full((nh * 8, HEAD_DIM), 0.125, F32)
@@ -388,16 +394,16 @@
         block = (tokens, width)
         square = (HEAD_DIM, HEAD_DIM)
         dma = pltpu.SemaphoreType.DMA
-        anywhere = pl.BlockSpec(memory_space=pl.ANY)
-        vmem = pl.BlockSpec(memory_space=pltpu.VMEM)
-        return pl.pallas_call(
+        anywhere = pl.BlockSpec(memory_space=pltpu.HBM)
+        operands = [
+            pltpu.with_memory_space_constraint(a, pltpu.HBM)
+            for a in (lq, lk, lv, ld, gate, gain.reshape(1, width), sq, sk, sv, seg)
+        ]
+        results = pl.pallas_call(
             functools.partial(kernel, n, nh),
             out_shape=[jax.ShapeDtypeStruct(block, BF16)] * 2,
-            in_specs=[anywhere] * 5
-            + [vmem]
-            + [anywhere] * 3
-            + [pl.BlockSpec(memory_space=pltpu.SMEM)],
-            out_specs=[vmem, vmem],
+            in_specs=[anywhere] * 10,
+            out_specs=[pl.BlockSpec(memory_space=pltpu.VMEM)] * 2,
             scratch_shapes=[
                 pltpu.VMEM(block, BF16),
                 pltpu.VMEM(block, BF16),
@@ -419,7 +425,9 @@
                 pltpu.VMEM((heads * tokens, 1), F32),
                 pltpu.VMEM((heads * tokens, HEAD_DIM), F32),
                 pltpu.VMEM((heads * tokens, 1), F32),
-                dma((8,)),
+                pltpu.VMEM((1, width), F32),
+                pltpu.SMEM((n,), jnp.int32),
+                dma((10,)),
                 dma((chips, 2)),
                 dma((2 * chips, 2)),
                 dma((chips, 2)),
@@ -439,7 +447,8 @@
                 has_side_effects=True,
                 vmem_limit_bytes=40 * 1024 * 1024,
             ),
-        )(lq, lk, lv, ld, gate, gain.reshape(1, width), sq, sk, sv, seg)
+        )(*operands)
+        return tuple(results)
 
     return jax.shard_map(
         step,

time: 28.9 us -> 20 us (0.69)
  local copies, waits for them, and re-layouts: 9.52 us -> 1.31 us
  Pallas kernels: 18.4 us -> 17.9 us
    unnamed x22 -> x2, local copies, waits for them, and re-layouts: 9.52 us -> 1.31 us
    pallas_call x1, Pallas kernels: 18.4 us -> 17.9 us  [step(): pl.pallas_call(functools.partial(kernel, n, nh), out_shape=[jax.ShapeDtyp...]
where the time goes in v3:
time: 20 us; the launch traced here: 19.8 us
  Pallas kernels  17.9 us (89%)
  local copies, waits for them, and re-layouts  1.31 us (7%)
  between operations  0.64 us (3%)
    pallas_call x1, Pallas kernels, step(): pl.pallas_call(functools.partial(kernel, n, nh), out_shape=[jax.ShapeDtyp...  17.9 us
    unnamed x2, local copies, waits for them, and re-layouts  1.31 us

profile of v3, /device:TPU:7, one launch (start us, length us, event | category | flops | bytes accessed | tf_op | source)
XLA Modules:
  0.0 19.8 jit_solution(7729547132239583096)
XLA Ops:
  0.6 17.9 %shard_map.113 = (bf16[128,512]{1,0:T(8,128)(2,1)S(1)}, bf16[128,512]{1,0:T(8,128)(2,1)S(1)}) custom-call(bf16[128,512]{1,0:T(8,128)(2,1)} %lq_hbm.1, bf16[128,512]{1,0:T(8,128)(2,1)} %lk_hbm.1, bf16[128,512]{1,0:T(8,128)(2,1)} %lv_hbm.1, f32[4,128]{1,0:T(4,128)} %ld_hbm.1, bf16[128,512]{1,0:T(8,128)(2,1)} %gate_hbm.1, f32[1,512]{1,0:T(1,128)} %bitcast.1, ...), custom_call_target="tpu_custom_call" | custom-call | tf_op jit(solution)/shard_map/pallas_call | solution.py:402
  18.5 0.7 %copy.14 = bf16[128,512]{1,0:T(8,128)(2,1)} copy(bf16[128,512]{1,0:T(8,128)(2,1)S(1)} %get-tuple-element.4) | data formatting | bytes 262144
  19.2 0.7 %copy.15 = bf16[128,512]{1,0:T(8,128)(2,1)} copy(bf16[128,512]{1,0:T(8,128)(2,1)S(1)} %get-tuple-element.5) | data formatting | bytes 262144

commit v4 on v3

--- a/solution.py
+++ b/solution.py
@@ -10,6 +10,7 @@
 HEAD_DIM = 128
 Q_PER_KV = 8
 NORM_EPS = 1e-06
+LOG2E = 1.4426950408889634
 MESH = pl.DeviceIdType.MESH
 F32 = jnp.float32
 BF16 = jnp.bfloat16
@@ -134,46 +135,6 @@
         )
 
     get_ld.wait()
-    get_sk.wait()
-    get_sv.wait()
-    pl.semaphore_wait(barrier, n - 1 + nh - 1)
-
-    def log_copy(i):
-        return remote(
-            logs.at[me],
-            logs.at[me],
-            log_send.at[i],
-            log_recv.at[i],
-            (me + 1 + i) % n,
-            col,
-        )
-
-    def kv_copy(i, part, to):
-        return remote(
-            kv.at[me, part],
-            kv.at[me, part],
-            kv_send.at[i, part],
-            kv_recv.at[i, part],
-            to,
-            col,
-        )
-
-    def far(i):
-        return ((chip + 1 + i) % chips) * 2 + core
-
-    def near(i):
-        return (chip + chips - 1 - i) % chips
-
-    each(n - 1, lambda i: log_copy(i).start())
-
-    def kv_go(i):
-        kv_copy(i, 0, far(i)).start()
-        kv_copy(i, 1, far(i)).start()
-
-    each(chips - 1, kv_go)
-    kv_copy(chips - 1, 0, sib).start()
-    kv_copy(chips - 1, 1, sib).start()
-
     rows = lax.broadcasted_iota(jnp.int32, (tokens, tokens), 0)
     cols = lax.broadcasted_iota(jnp.int32, (tokens, tokens), 1)
     causal = rows >= cols
@@ -183,6 +144,46 @@
     cum_col = dot(lower, decay, NT, HIGH)
     tail = jnp.exp(cum_col[tokens - 1 : tokens, :] - cum_col)
     lift = jnp.exp(cum_col)
+
+    get_sk.wait()
+    get_sv.wait()
+    pl.semaphore_wait(barrier, n - 1 + nh - 1)
+
+    def log_copy(i):
+        return remote(
+            logs.at[me],
+            logs.at[me],
+            log_send.at[i],
+            log_recv.at[i],
+            (me + 1 + i) % n,
+            col,
+        )
+
+    def kv_copy(i, part, to):
+        return remote(
+            kv.at[me, part],
+            kv.at[me, part],
+            kv_send.at[i, part],
+            kv_recv.at[i, part],
+            to,
+            col,
+        )
+
+    def far(i):
+        return ((chip + 1 + i) % chips) * 2 + core
+
+    def near(i):
+        return (chip + chips - 1 - i) % chips
+
+    each(n - 1, lambda i: log_copy(i).start())
+
+    def kv_go(i):
+        kv_copy(i, 0, far(i)).start()
+        kv_copy(i, 1, far(i)).start()
+
+    each(chips - 1, kv_go)
+    kv_copy(chips - 1, 0, sib).start()
+    kv_copy(chips - 1, 1, sib).start()
 
     def cut(h):
         return slice(h * HEAD_DIM, (h + 1) * HEAD_DIM)
@@ -237,38 +238,56 @@
 
     each(chips, tot_go)
 
-    scale = HEAD_DIM ** (-0.5)
+    scale = HEAD_DIM ** (-0.5) * LOG2E
     get_seg.wait()
     own_segment = seg_ref[me]
     get_sq.wait()
     for h in range(heads):
         qs[h * tokens : (h + 1) * tokens, :] = sq[:, cut(h)]
-
-    def soft_first():
-        logits = dot(qs[...], kv[me, 0], NT) * scale
-        shape = (heads, tokens, tokens)
-        logits = jnp.where(causal[None], logits.reshape(shape), -1e30).reshape(
-            heads * tokens, tokens
-        )
-        peak = jnp.max(logits, axis=1, keepdims=True)
-        weights = jnp.exp(logits - peak)
+    ones = jnp.ones((tokens, HEAD_DIM), BF16)
+
+    def soft_group(owners, first=False):
+        keys = jnp.concatenate([kv[o, 0] for o in owners], axis=0)
+        values = jnp.concatenate(
+            [jnp.concatenate([kv[o, 1], ones], axis=1) for o in owners], axis=0
+        )
+        raw = dot(qs[...], keys, NT)
+        logits = []
+        for j, owner in enumerate(owners):
+            part = raw[:, j * tokens : (j + 1) * tokens] * scale
+            if first and j == 0:
+                shape = (heads, tokens, tokens)
+                part = jnp.where(causal[None], part.reshape(shape), -1e30)
+                part = part.reshape(heads * tokens, tokens)
+            else:
+                shown = seg_ref[owner] < own_segment
+                part = part + jnp.where(shown, 0.0, -1e30).astype(F32)
+            logits.append(part)
+        peak = jnp.max(functools.reduce(jnp.maximum, logits), axis=1, keepdims=True)
+        peak = jnp.broadcast_to(peak, (heads * tokens, HEAD_DIM))
+        if not first:
+            old = top[...]
+            peak = jnp.maximum(old, peak)
+            fade = jnp.exp2(old - peak)
+        weights = [jnp.exp2(part - peak).astype(BF16) for part in logits]
+        both = dot(jnp.concatenate(weights, axis=1), values)
         top[...] = peak
-        den[...] = jnp.sum(weights, axis=1, keepdims=True)
-        acc[...] = dot(weights.astype(BF16), kv[me, 1])
-
-    def soft_next(owner):
-        shown = seg_ref[owner] < own_segment
-        bias = jnp.where(shown, 0.0, -1e30).astype(F32)
-        logits = dot(qs[...], kv[owner, 0], NT) * scale + bias
-        old = top[...]
-        peak = jnp.maximum(old, jnp.max(logits, axis=1, keepdims=True))
-        fade = jnp.exp(old - peak)
-        weights = jnp.exp(logits - peak)
-        top[...] = peak
-        den[...] = den[...] * fade + jnp.sum(weights, axis=1, keepdims=True)
-        acc[...] = acc[...] * fade + dot(weights.astype(BF16), kv[owner, 1])
-
-    soft_first()
+        if first:
+            acc[...] = both[:, :HEAD_DIM]
+            den[...] = both[:, HEAD_DIM:]
+        else:
+            acc[...] = acc[...] * fade + both[:, :HEAD_DIM]
+            den[...] = den[...] * fade + both[:, HEAD_DIM:]
+
+    def soft_rest(other):
+        if chips <= 5:
+            soft_group([near(i) * 2 + other for i in range(chips - 1)])
+        else:
+            each(chips - 1, lambda i: soft_group([near(i) * 2 + other]))
+
+    kv_copy(chips - 1, 0, sib).wait_recv()
+    kv_copy(chips - 1, 1, sib).wait_recv()
+    soft_group([me, sib], True)
 
     def fwd_copy(i, part, owner):
         return remote(
@@ -281,11 +300,9 @@
         )
 
     def kv_pass(i):
-        owner = near(i) * 2 + core
         for part in range(2):
             kv_copy(i, part, far(i)).wait_recv()
-            fwd_copy(i, part, owner).start()
-        soft_next(owner)
+            fwd_copy(i, part, near(i) * 2 + core).start()
 
     each(chips - 1, kv_pass)
 
@@ -305,9 +322,7 @@
     ent_copy = remote(ent_own, ent_sib, ent_send, ent_recv, sib, col)
     ent_copy.start()
 
-    kv_copy(chips - 1, 0, sib).wait_recv()
-    kv_copy(chips - 1, 1, sib).wait_recv()
-    soft_next(sib)
+    soft_rest(core)
 
     even_decay = jnp.exp(total(chip * 2))
     ent_copy.wait_recv()
@@ -338,25 +353,25 @@
     def kv_last(i):
         for part in range(2):
             fwd_copy(i, part, near(i) * 2 + core).wait_recv()
-        soft_next(near(i) * 2 + 1 - core)
 
     each(chips - 1, kv_last)
+    soft_rest(1 - core)
     for h in range(heads):
         r = slice(h * tokens, (h + 1) * tokens)
         soft_ref[:, cut(h)] = (acc[r, :] / den[r, :]).astype(BF16)
 
     get_gate.wait()
     get_gain.wait()
+    for h in range(heads):
+        opened = jax.nn.sigmoid(gate[:, cut(h)].astype(F32))
+        mixed[:, cut(h)] = mixed[:, cut(h)] * (gain_ref[:, cut(h)] * opened)
     each(nh - 1, lambda i: sum_copy(i).wait_recv())
     everyone = sums[...].reshape(nh * 8, tokens)
     eighth = jnp.full((nh * 8, HEAD_DIM), 0.125, F32)
     spread_sums = dot(everyone, eighth, TN, HIGH)
     inverse = lax.rsqrt(spread_sums / (heads * HEAD_DIM * nh) + NORM_EPS)
     for h in range(heads):
-        opened = jax.nn.sigmoid(gate[:, cut(h)].astype(F32))
-        lin_ref[:, cut(h)] = (mixed[:, cut(h)] * inverse * gain_ref[:, cut(h)] * opened).astype(
-            BF16
-        )
+        lin_ref[:, cut(h)] = (mixed[:, cut(h)] * inverse).astype(BF16)
 
     each(n - 1, lambda i: log_copy(i).wait_send())
 
@@ -422,9 +437,9 @@
                 pltpu.VMEM((half,) + square, BF16),
                 pltpu.VMEM(block, F32),
                 pltpu.VMEM((nh, 8, tokens), F32),
-                pltpu.VMEM((heads * tokens, 1), F32),
                 pltpu.VMEM((heads * tokens, HEAD_DIM), F32),
-                pltpu.VMEM((heads * tokens, 1), F32),
+                pltpu.VMEM((heads * tokens, HEAD_DIM), F32),
+                pltpu.VMEM((heads * tokens, HEAD_DIM), F32),
                 pltpu.VMEM((1, width), F32),
                 pltpu.SMEM((n,), jnp.int32),
                 dma((10,)),

time: 20 us -> 19.8 us (0.990)
  Pallas kernels: 17.9 us -> 17.6 us
    pallas_call x1, Pallas kernels: 17.9 us -> 17.6 us  [step(): pl.pallas_call(functools.partial(kernel, n, nh), out_shape=[jax.ShapeDtyp...]
where the time goes in v4:
time: 19.8 us; the launch traced here: 19.5 us
  Pallas kernels  17.6 us (89%)
  local copies, waits for them, and re-layouts  1.31 us (7%)
  between operations  0.64 us (3%)
    pallas_call x1, Pallas kernels, step(): pl.pallas_call(functools.partial(kernel, n, nh), out_shape=[jax.ShapeDtyp...  17.6 us
    unnamed x2, local copies, waits for them, and re-layouts  1.31 us

profile of v4, /device:TPU:7, one launch (start us, length us, event | category | flops | bytes accessed | tf_op | source)
XLA Modules:
  0.0 19.5 jit_solution(16959195021726378997)
XLA Ops:
  0.6 17.6 %shard_map.113 = (bf16[128,512]{1,0:T(8,128)(2,1)S(1)}, bf16[128,512]{1,0:T(8,128)(2,1)S(1)}) custom-call(bf16[128,512]{1,0:T(8,128)(2,1)} %lq_hbm.1, bf16[128,512]{1,0:T(8,128)(2,1)} %lk_hbm.1, bf16[128,512]{1,0:T(8,128)(2,1)} %lv_hbm.1, f32[4,128]{1,0:T(4,128)} %ld_hbm.1, bf16[128,512]{1,0:T(8,128)(2,1)} %gate_hbm.1, f32[1,512]{1,0:T(1,128)} %bitcast.1, ...), custom_call_target="tpu_custom_call" | custom-call | tf_op jit(solution)/shard_map/pallas_call | solution.py:417
  18.2 0.7 %copy.14 = bf16[128,512]{1,0:T(8,128)(2,1)} copy(bf16[128,512]{1,0:T(8,128)(2,1)S(1)} %get-tuple-element.4) | data formatting | bytes 262144
  18.9 0.7 %copy.15 = bf16[128,512]{1,0:T(8,128)(2,1)} copy(bf16[128,512]{1,0:T(8,128)(2,1)S(1)} %get-tuple-element.5) | data formatting | bytes 262144

commit v5 on v4

--- a/solution.py
+++ b/solution.py
@@ -149,15 +149,19 @@
     get_sv.wait()
     pl.semaphore_wait(barrier, n - 1 + nh - 1)
 
-    def log_copy(i):
+    def log_copy(send, recv, to):
         return remote(
-            logs.at[me],
-            logs.at[me],
-            log_send.at[i],
-            log_recv.at[i],
-            (me + 1 + i) % n,
-            col,
-        )
+            logs.at[me], logs.at[me], log_send.at[send], log_recv.at[recv], to, col
+        )
+
+    def log_far(i, other):
+        to = ((chip + 1 + i) % chips) * 2 + other
+        return log_copy(2 * i + other, 2 * i + core, to)
+
+    def log_came(i, other):
+        return log_copy(2 * i, 2 * i + other, sib)
+
+    log_near = log_copy(n - 1, n - 1, sib)
 
     def kv_copy(i, part, to):
         return remote(
@@ -175,7 +179,7 @@
     def near(i):
         return (chip + chips - 1 - i) % chips
 
-    each(n - 1, lambda i: log_copy(i).start())
+    log_near.start()
 
     def kv_go(i):
         kv_copy(i, 0, far(i)).start()
@@ -195,6 +199,12 @@
         mem_own[h] = dot(weighted, lv[:, cut(h)], TN).astype(BF16)
     mem_copy = remote(mem_own, mem_sib, mem_send, mem_recv, sib, col)
     mem_copy.start()
+
+    def log_go(i):
+        log_far(i, 0).start()
+        log_far(i, 1).start()
+
+    each(chips - 1, log_go)
 
     get_lq.wait()
     for h in range(heads):
@@ -204,7 +214,7 @@
         mixing = (scores * weight).astype(BF16)
         mixed[:, cut(h)] = dot(mixing, lv[:, cut(h)])
 
-    each(n - 1, lambda i: log_copy(i).wait_recv())
+    log_near.wait_recv()
 
     def total(i):
         return jnp.sum(logs[i], axis=1, keepdims=True)
@@ -306,6 +316,11 @@
 
     each(chips - 1, kv_pass)
 
+    def log_get(i):
+        log_came(i, 0).wait_recv()
+        log_came(i, 1).wait_recv()
+
+    each(chips - 1, log_get)
     pre[...] = jnp.zeros_like(pre)
 
     def join(i):
@@ -373,7 +388,13 @@
     for h in range(heads):
         lin_ref[:, cut(h)] = (mixed[:, cut(h)] * inverse).astype(BF16)
 
-    each(n - 1, lambda i: log_copy(i).wait_send())
+    log_near.wait_send()
+
+    def log_sent(i):
+        log_far(i, 0).wait_send()
+        log_far(i, 1).wait_send()
+
+    each(chips - 1, log_sent)
 
     def kv_sent(i):
         for part in range(2):

time: 19.8 us -> 19.8 us (level)
  no operation moved by 1% of the time
where the time goes in v5:
time: 19.8 us; the launch traced here: 19.5 us
  Pallas kernels  17.6 us (89%)
  local copies, waits for them, and re-layouts  1.31 us (7%)
  between operations  0.64 us (3%)
    pallas_call x1, Pallas kernels, step(): pl.pallas_call(functools.partial(kernel, n, nh), out_shape=[jax.ShapeDtyp...  17.6 us
    unnamed x2, local copies, waits for them, and re-layouts  1.31 us

profile of v5, /device:TPU:7, one launch (start us, length us, event | category | flops | bytes accessed | tf_op | source)
XLA Modules:
  0.0 19.5 jit_solution(14457550810306863244)
XLA Ops:
  0.6 17.6 %shard_map.113 = (bf16[128,512]{1,0:T(8,128)(2,1)S(1)}, bf16[128,512]{1,0:T(8,128)(2,1)S(1)}) custom-call(bf16[128,512]{1,0:T(8,128)(2,1)} %lq_hbm.1, bf16[128,512]{1,0:T(8,128)(2,1)} %lk_hbm.1, bf16[128,512]{1,0:T(8,128)(2,1)} %lv_hbm.1, f32[4,128]{1,0:T(4,128)} %ld_hbm.1, bf16[128,512]{1,0:T(8,128)(2,1)} %gate_hbm.1, f32[1,512]{1,0:T(1,128)} %bitcast.1, ...), custom_call_target="tpu_custom_call" | custom-call | tf_op jit(solution)/shard_map/pallas_call | solution.py:438
  18.2 0.7 %copy.14 = bf16[128,512]{1,0:T(8,128)(2,1)} copy(bf16[128,512]{1,0:T(8,128)(2,1)S(1)} %get-tuple-element.4) | data formatting | bytes 262144
  18.9 0.7 %copy.15 = bf16[128,512]{1,0:T(8,128)(2,1)} copy(bf16[128,512]{1,0:T(8,128)(2,1)S(1)} %get-tuple-element.5) | data formatting | bytes 262144

commit v6 on v5

--- a/solution.py
+++ b/solution.py
@@ -314,7 +314,6 @@
             kv_copy(i, part, far(i)).wait_recv()
             fwd_copy(i, part, near(i) * 2 + core).start()
 
-    each(chips - 1, kv_pass)
 
     def log_get(i):
         log_came(i, 0).wait_recv()
@@ -336,6 +335,7 @@
     ent_own[...] = pre[...].astype(BF16)
     ent_copy = remote(ent_own, ent_sib, ent_send, ent_recv, sib, col)
     ent_copy.start()
+    each(chips - 1, kv_pass)
 
     soft_rest(core)
 

time: 19.8 us -> 19.8 us (level)
  no operation moved by 1% of the time
where the time goes in v6:
time: 19.8 us; the launch traced here: 19.5 us
  Pallas kernels  17.6 us (89%)
  local copies, waits for them, and re-layouts  1.31 us (7%)
  between operations  0.64 us (3%)
    pallas_call x1, Pallas kernels, step(): pl.pallas_call(functools.partial(kernel, n, nh), out_shape=[jax.ShapeDtyp...  17.6 us
    unnamed x2, local copies, waits for them, and re-layouts  1.31 us

profile of v6, /device:TPU:7, one launch (start us, length us, event | category | flops | bytes accessed | tf_op | source)
XLA Modules:
  0.0 19.5 jit_solution(5291661233499443784)
XLA Ops:
  0.6 17.6 %shard_map.113 = (bf16[128,512]{1,0:T(8,128)(2,1)S(1)}, bf16[128,512]{1,0:T(8,128)(2,1)S(1)}) custom-call(bf16[128,512]{1,0:T(8,128)(2,1)} %lq_hbm.1, bf16[128,512]{1,0:T(8,128)(2,1)} %lk_hbm.1, bf16[128,512]{1,0:T(8,128)(2,1)} %lv_hbm.1, f32[4,128]{1,0:T(4,128)} %ld_hbm.1, bf16[128,512]{1,0:T(8,128)(2,1)} %gate_hbm.1, f32[1,512]{1,0:T(1,128)} %bitcast.1, ...), custom_call_target="tpu_custom_call" | custom-call | tf_op jit(solution)/shard_map/pallas_call | solution.py:438
  18.2 0.7 %copy.14 = bf16[128,512]{1,0:T(8,128)(2,1)} copy(bf16[128,512]{1,0:T(8,128)(2,1)S(1)} %get-tuple-element.4) | data formatting | bytes 262144
  18.9 0.7 %copy.15 = bf16[128,512]{1,0:T(8,128)(2,1)} copy(bf16[128,512]{1,0:T(8,128)(2,1)S(1)} %get-tuple-element.5) | data formatting | bytes 262144
